TPU v7x, 256 devices: a whole 4x4x8 slice. The times are simulated.
256 devices in a mesh: rep: 8 (over z), own: 32 (over x, y, core).
Axes of the slice: x: 4, y: 4, z: 8, core: 2. Of those that a mesh axis runs over, the one named last changes fastest.
Arguments:
- grads: bfloat16 [8, 192, 512, 512], P('rep', None, 'own'), may hold values from -6 to 6
- slot_of: int32 [192], P('rep'), may hold values from 0 to 31, as said below
- left_stats: float32 [8, 32, 512, 512], P('rep', 'own'), may hold values from -6 to 6
- right_stats: float32 [8, 32, 512, 512], P('rep', 'own'), may hold values from -6 to 6
- left_roots: bfloat16 [8, 32, 512, 512], P('rep', 'own'), may hold values from -0.25 to 0.25
- right_roots: bfloat16 [8, 32, 512, 512], P('rep', 'own'), may hold values from -0.25 to 0.25
Outputs:
- left_new: float32 [8, 32, 512, 512], P('rep', 'own')
- right_new: float32 [8, 32, 512, 512], P('rep', 'own')
- update: float32 [192, 512, 512], P('rep', 'own')
Inputs may be any that keep to these rules, and one draw needn't show every extreme that they name: `slot_of`: within each aligned run of 24 blocks (one group) the values are distinct; the value is the index along `own` of the device that keeps the block's statistics (each owner keeps exactly one slot); in every group 32 - 24 slots hold no block.
All inputs are finite; a program needn't handle non-finite values.
Results may differ from a plain program's by a relative error of at most 0.02.
Values may be sent and summed in bfloat16 or wider, within the bound.
No kernel may reach another device: no remote copies, remote signals or barrier semaphores. Data moves between devices by JAX's collectives and lax.ppermute only.
A program may use at most 128 MiB of HBM per device.

v0:
```python
import jax
import jax.numpy as jnp
from jax import lax
from jax.sharding import PartitionSpec as P

DECAY = 0.99
EPSILON = 1e-06


def precondition(block, left, right, left_root, right_root):
    gram_left = jnp.einsum("ik,jk->ij", block, block, preferred_element_type=jnp.float32)
    gram_right = jnp.einsum("ki,kj->ij", block, block, preferred_element_type=jnp.float32)
    left_next = DECAY * left + (1.0 - DECAY) * gram_left
    right_next = DECAY * right + (1.0 - DECAY) * gram_right
    half = jnp.dot(left_root, block, preferred_element_type=jnp.float32).astype(jnp.bfloat16)
    precond = jnp.dot(half, right_root, preferred_element_type=jnp.float32)
    wide = block.astype(jnp.float32)
    ratio = jnp.sqrt(jnp.mean(wide * wide) + EPSILON) / jnp.sqrt(
        jnp.mean(precond * precond) + EPSILON
    )
    return (left_next, right_next, precond * ratio)


def local(grads, slot_of, left_stats, right_stats, left_roots, right_roots):
    owners = lax.axis_size("own")
    local_terms = grads[0].astype(jnp.float32)
    total = lax.psum_scatter(
        local_terms.astype(jnp.bfloat16), "rep", scatter_dimension=0, tiled=True
    )
    group = total.shape[0]
    strip = total.shape[1]
    width = total.shape[2]
    slots_here = left_stats.shape[1]
    mine = lax.axis_index("own")
    picks = (slot_of[:, None] == mine * slots_here + jnp.arange(slots_here)[None, :]).astype(
        jnp.bfloat16
    )
    placed = jnp.einsum(
        "gc,gij->cij",
        picks,
        lax.all_gather(total, "own", axis=1, tiled=True),
        preferred_element_type=jnp.float32,
    ).astype(jnp.bfloat16)
    left_next, right_next, grafted = jax.vmap(precondition)(
        placed, left_stats[0], right_stats[0], left_roots[0], right_roots[0]
    )
    picks_wide = picks.astype(jnp.float32)
    split_steps = grafted.reshape(slots_here, owners, strip, width)
    many = group * lax.axis_size("own") // group
    term = jnp.einsum("gc,ckij->kgij", picks_wide, split_steps, precision=lax.Precision.HIGHEST)
    update = lax.psum_scatter(
        term.reshape(many * group, strip, width), "own", scatter_dimension=0, tiled=True
    )
    return (left_next[None], right_next[None], update)


def solution(mesh):
    return jax.shard_map(
        local,
        mesh=mesh,
        in_specs=(
            P("rep", None, "own", None),
            P("rep"),
            P("rep", "own", None, None),
            P("rep", "own", None, None),
            P("rep", "own", None, None),
            P("rep", "own", None, None),
        ),
        out_specs=(P("rep", "own", None, None), P("rep", "own", None, None), P("rep", "own", None)),
        check_vma=False,
    )
```

profile of v0, /device:TPU:1, one launch (start us, length us, event | category | flops | bytes accessed | tf_op | source)
XLA Modules:
  0.0 314.4 jit_solution(9849550604384714244)
XLA Ops:
  7.2 0.0 copy-start
  7.2 0.0 copy-start.3
  7.2 0.0 reduce-scatter.3.cloned.1.call-start
  7.2 0.7 reduce-scatter.3.cloned.1.call-update
  7.9 0.0 all-gather.2.cloned.1.call-start
  8.0 50.5 %reduce-scatter.3.cloned.1.call-done = bf16[24,16,512]{2,1,0:T(8,128)(2,1)} async-done(((bf16[192,16,512]{2,1,0:T(8,128)(2,1)}), bf16[24,16,512]{2,1,0:T(8,128)(2,1)}) %reduce-scatter.3.cloned.1.call-update) | async-done | bytes 393232 | tf_op jit(solution)/shard_map/reduce_scatter | solution.py:27
  58.5 0.0 all-gather.2.cloned.1.call-update
  58.5 0.0 reduce-scatter.5.cloned.1.call-start
  58.6 0.7 compare_convert_fusion
  59.2 72.2 %all-gather.2.cloned.1.call-done = bf16[24,512,512]{2,1,0:T(8,128)(2,1)} async-done(((bf16[24,16,512]{2,1,0:T(8,128)(2,1)}), bf16[24,512,512]{2,1,0:T(8,128)(2,1)}) %all-gather.2.cloned.1.call-update) | async-done | bytes 12582928 | tf_op jit(solution)/shard_map/all_gather | solution.py:41
  131.5 13.3 %fusion = bf16[1,512,512]{2,0,1:T(2,128)(2,1)S(1)} fusion(bf16[24,512,512]{2,1,0:T(8,128)(2,1)} %all-gather.2.cloned.1.call-done, s32[24]{0:T(128)} %param.7, s32[]{:T(128)S(6)} %axis_index.12), kind=kOutput, calls=%fused_computation | convolution fusion | flops 12582936 | bytes 13107300 | tf_op jit(solution)/shard_map/gc,gij->cij/dot_general | solution.py:38
  144.8 0.9 multiply_reduce_fusion.1
  145.7 0.0 copy-done
  145.7 0.0 copy-done.3
  145.7 1.6 multiply_reduce_fusion
  148.7 0.1 broadcast_multiply_fusion.1
  148.8 11.6 %broadcast_multiply_fusion = f32[32,16,512,24]{2,1,3,0:T(8,128)} fusion(f32[24]{0:T(128)S(1)} %compare_convert_fusion, f32[32,16,512]{2,1,0:T(8,128)S(1)} %bitcast.36), kind=kLoop, calls=%fused_computation.2 | loop fusion | flops 6291456 | bytes 26214496 | tf_op jit(solution)/shard_map/gc,ckij->kgij/dot_general | solution.py:50
  160.4 0.0 copy-start.1
  160.4 0.0 copy-start.2
  160.4 0.0 reduce-scatter.5.cloned.1.call-update
  160.5 1.2 copy-done.1
  161.7 1.4 fusion.5
  163.1 0.0 copy-done.2
  163.1 1.5 fusion.3
  164.6 143.3 %reduce-scatter.5.cloned.1.call-done = f32[24,16,512]{2,1,0:T(8,128)} async-done(((f32[768,16,512]{2,1,0:T(8,128)}), f32[24,16,512]{2,1,0:T(8,128)}) %reduce-scatter.5.cloned.1.call-update) | async-done | bytes 786448 | tf_op jit(solution)/shard_map/reduce_scatter | solution.py:51
Async XLA Ops:
  7.2 138.5 %copy-start = (bf16[1,1,512,512]{3,2,1,0:T(8,128)(2,1)S(1)}, bf16[1,1,512,512]{3,2,1,0:T(8,128)(2,1)}, u32[]{:S(2)}) copy-start(bf16[1,1,512,512]{3,2,1,0:T(8,128)(2,1)} %param.11) | copy-start | bytes 1572868
  7.2 138.5 %copy-start.3 = (bf16[1,1,512,512]{3,2,1,0:T(8,128)(2,1)S(1)}, bf16[1,1,512,512]{3,2,1,0:T(8,128)(2,1)}, u32[]{:S(2)}) copy-start(bf16[1,1,512,512]{3,2,1,0:T(8,128)(2,1)} %param.10) | copy-start | bytes 1572868
  7.2 51.3 %reduce-scatter.3.cloned.1.call-start = ((), (), s32[]{:S(2)}) async-start(), calls=%async_computation.2 | async-start | bytes 3538944 | tf_op jit(solution)/shard_map/reduce_scatter | solution.py:27
  7.9 123.6 %all-gather.2.cloned.1.call-start = ((), (), s32[]{:S(2)}) async-start(), calls=%async_computation.3 | async-start | bytes 12976128 | tf_op jit(solution)/shard_map/all_gather | solution.py:41
  58.5 249.4 %reduce-scatter.5.cloned.1.call-start = ((), (), s32[]{:S(2)}) async-start(), calls=%async_computation.4 | async-start | bytes 25952256 | tf_op jit(solution)/shard_map/reduce_scatter | solution.py:51
  160.4 1.2 copy-start.1
  160.4 2.7 copy-start.2
Sparse Core Ops, SparseCore 0:
  10.6 47.8 reduce-scatter.2
  61.2 70.2 all-gather.1
  160.6 147.2 reduce-scatter.4
where the time goes:
time: 315 us; the launch traced here: 314 us
  waiting for transfers between devices  267 us (85%)
  matrix products  17.8 us (6%)
  between operations  15.2 us (5%)
  other arithmetic  13.3 us (4%)
    reduce_scatter x1, waiting for transfers between devices, local(): lax.psum_scatter(term.reshape(many * group, strip, width), 'own', scatter...  143 us
    all_gather x1, waiting for transfers between devices, local(): lax.all_gather(total, 'own', axis=1, tiled=True)  72.2 us
    reduce_scatter x1, waiting for transfers between devices, local(): lax.psum_scatter(local_terms.astype(jnp.bfloat16), 'rep', scatter_dimensi...  50.5 us
    dot_general x1, matrix products, local(): jnp.einsum('gc,gij->cij', picks, lax.all_gather(total, 'own', axis=1, til...  13.3 us
    dot_general x1, other arithmetic, local(): jnp.einsum('gc,ckij->kgij', picks_wide, split_steps, precision=lax.Precis...  11.6 us
  transfers between devices with their start and end apart: 3, of which 3 were waited for; matrix products, arithmetic and copies ran while one was open for 1% of the time, Pallas kernels for 0%

commit v1 on v0

v1 whole, which is shorter than its diff:
```python
import jax
import jax.numpy as jnp
from jax import lax
from jax.sharding import PartitionSpec as P

DECAY = 0.99
EPSILON = 1e-06


def reduce_to_group(grads, replicas):
    me = lax.axis_index("rep")
    reach = replicas // 2
    groups = grads.reshape((replicas, -1) + grads.shape[1:])
    cut = groups.shape[1] // 2
    ahead = [(i, (i + 1) % replicas) for i in range(replicas)]
    back = [(i, (i - 1) % replicas) for i in range(replicas)]

    def mine(group):
        return lax.dynamic_index_in_dim(groups, (group + replicas) % replicas, 0, False)

    far = mine(me + reach)
    down = lax.ppermute(far[:cut], "rep", back)
    up = lax.ppermute(far[cut:], "rep", ahead)
    for step in range(reach - 1, 0, -1):
        own_down, own_up = mine(me - step), mine(me + step)
        if step == reach - 1:
            down = jnp.concatenate([own_down[:cut] + down, own_down[cut:]], 0)
            up = jnp.concatenate([own_up[:cut], own_up[cut:] + up], 0)
        else:
            down, up = down + own_down, up + own_up
        down = lax.ppermute(down, "rep", back)
        up = lax.ppermute(up, "rep", ahead)
    wide = down.astype(jnp.float32) + up.astype(jnp.float32) + mine(me).astype(jnp.float32)
    return wide.astype(jnp.bfloat16)


def local(grads, slot_of, left_stats, right_stats, left_roots, right_roots):
    replicas, owners = lax.axis_size("rep"), lax.axis_size("own")
    total = reduce_to_group(grads[0], replicas)
    group, strip, width = total.shape
    block_size = strip * owners

    picks = slot_of[:, None] == jnp.arange(owners)[None, :]
    sends = jnp.einsum(
        "gc,gij->cij", picks.astype(jnp.bfloat16), total, preferred_element_type=jnp.float32
    ).astype(jnp.bfloat16)
    block = lax.all_to_all(sends, "own", 0, 0, tiled=True).reshape(block_size, width)

    half = jnp.dot(left_roots[0, 0], block, preferred_element_type=jnp.float32)
    precond = jnp.dot(
        half.astype(jnp.bfloat16), right_roots[0, 0], preferred_element_type=jnp.float32
    )
    wide = block.astype(jnp.float32)
    ratio = jnp.sqrt(jnp.mean(wide * wide) + EPSILON) / jnp.sqrt(
        jnp.mean(precond * precond) + EPSILON
    )
    grafted = (precond * ratio).astype(jnp.bfloat16).reshape(owners, strip, width)
    rows = lax.all_to_all(grafted, "own", 0, 0, tiled=True)

    gram_left = jnp.einsum("ik,jk->ij", block, block, preferred_element_type=jnp.float32)
    gram_right = jnp.einsum("ki,kj->ij", block, block, preferred_element_type=jnp.float32)
    left_next = DECAY * left_stats[0, 0] + (1.0 - DECAY) * gram_left
    right_next = DECAY * right_stats[0, 0] + (1.0 - DECAY) * gram_right

    update = jnp.einsum(
        "gc,cij->gij", picks.astype(jnp.bfloat16), rows, preferred_element_type=jnp.float32
    )
    return left_next[None, None], right_next[None, None], update


def solution(mesh):
    return jax.shard_map(
        local,
        mesh=mesh,
        in_specs=(
            P("rep", None, "own", None),
            P("rep"),
            P("rep", "own", None, None),
            P("rep", "own", None, None),
            P("rep", "own", None, None),
            P("rep", "own", None, None),
        ),
        out_specs=(P("rep", "own", None, None), P("rep", "own", None, None), P("rep", "own", None)),
        check_vma=False,
    )
```

time: 315 us -> 93.4 us (0.30)
  waiting for transfers between devices: 267 us -> 33.1 us
  blocking collectives: 0 us -> 23.1 us
  starting transfers between devices: 0.11 us -> 21 us
  between operations: 15.2 us -> 2.33 us
  matrix products: 17.8 us -> 6.62 us
  other arithmetic: 13.3 us -> 3.18 us
    reduce_scatter x2 -> x0, waiting for transfers between devices: 194 us -> none  [the longest x1 143 us: local(): lax.psum_scatter(term.reshape(many * group, strip, width), 'own', scatter...]
    all_gather x1 -> x0, waiting for transfers between devices: 72.2 us -> none  [local(): lax.all_gather(total, 'own', axis=1, tiled=True)]
    ppermute x0 -> x8, waiting for transfers between devices: none -> 24.5 us  [the longest x3 16.6 us: reduce_to_group(): down = lax.ppermute(down, 'rep', back)]
    all_to_all x0 -> x1, blocking collectives: none -> 23.1 us  [local(): lax.all_to_all(sends, 'own', 0, 0, tiled=True).reshape(block_size, width)]
    ppermute x0 -> x8, starting transfers between devices: none -> 17.3 us  [the longest x3 10.5 us: reduce_to_group(): down = lax.ppermute(down, 'rep', back)]
    dot_general x1 -> x0, other arithmetic: 11.6 us -> none  [local(): jnp.einsum('gc,ckij->kgij', picks_wide, split_steps, precision=lax.Precis...]
    dot_general x4 -> x5, matrix products: 17.8 us -> 6.62 us  [the longest x1 2.75 us: local(): jnp.dot(half.astype(jnp.bfloat16), right_roots[0, 0], preferred_element_t...]
    all_to_all x0 -> x1, waiting for transfers between devices: none -> 8.66 us  [local(): rows = lax.all_to_all(grafted, 'own', 0, 0, tiled=True)]
  transfers between devices with their start and end apart: 3 -> 9, of which waited for: 3 -> 6; matrix products, arithmetic and copies ran while one was open for 1% -> 5% of each run, Pallas kernels for 0% -> 0%
where the time goes in v1:
time: 93.4 us; the launch traced here: 93.1 us
  waiting for transfers between devices  33.1 us (35%)
  blocking collectives  23.1 us (25%)
  starting transfers between devices  21 us (22%)
  matrix products  6.62 us (7%)
  local copies, waits for them, and re-layouts  3.8 us (4%)
  other arithmetic  3.18 us (3%)
  between operations  2.33 us (2%)
    all_to_all x1, blocking collectives, local(): lax.all_to_all(sends, 'own', 0, 0, tiled=True).reshape(block_size, width)  23.1 us
    ppermute x3, waiting for transfers between devices, reduce_to_group(): down = lax.ppermute(down, 'rep', back)  16.6 us
    ppermute x3, starting transfers between devices, reduce_to_group(): down = lax.ppermute(down, 'rep', back)  10.5 us
    all_to_all x1, waiting for transfers between devices, local(): rows = lax.all_to_all(grafted, 'own', 0, 0, tiled=True)  8.66 us
    ppermute x1, starting transfers between devices, reduce_to_group(): down = lax.ppermute(far[:cut], 'rep', back)  6.48 us
    ppermute x1, waiting for transfers between devices, reduce_to_group(): down = lax.ppermute(far[:cut], 'rep', back)  4.42 us
    all_to_all x1, starting transfers between devices, local(): rows = lax.all_to_all(grafted, 'own', 0, 0, tiled=True)  3.68 us
    ppermute x3, waiting for transfers between devices, reduce_to_group(): up = lax.ppermute(up, 'rep', ahead)  3.45 us
  transfers between devices with their start and end apart: 9, of which 6 were waited for; matrix products, arithmetic and copies ran while one was open for 5% of the time, Pallas kernels for 0%

profile of v1, /device:TPU:1, one launch (start us, length us, event | category | flops | bytes accessed | tf_op | source)
XLA Modules:
  0.0 93.1 jit_solution(17919778092808111056)
XLA Ops:
  0.6 0.0 copy-start
  0.7 1.5 %constant_dynamic-slice_fusion.2 = (bf16[1,12,16,512]{3,2,1,0:T(8,128)(2,1)S(1)}, bf16[1,12,16,512]{3,2,1,0:T(8,128)(2,1)S(1)}, bf16[1,12,16,512]{3,2,1,0:T(8,12...) fusion(bf16[8,24,16,512]{3,2,1,0:T(8,128)(2,1)} %bitcast.75, ...), kind=kLoop, calls=%fused_computation.40 | loop fusion | bytes 2359312 | tf_op jit(solution)/shard_map/slice | solution.py:27
  2.2 0.1 copy.78
  2.3 6.5 %collective-permute-start = (bf16[12,16,512]{2,0,1:T(8,128)(2,1)S(1)}, bf16[12,16,512]{2,0,1:T(8,128)(2,1)S(1)}, u32[]{:S(2)}, u32[]{:S(2)}) collective-permute-start(bf16[12,16,512]{2,0,1:T(8,128)(2,1)S(1)} %bitcast.80), channel_id=1, source_target_pairs={{0,224},{32,0},{64,32},{96,64},{128,96},{160,128},{192,160},{224,1... | collective-permute-start | bytes 589832 | tf_op jit(solution)/shard_map/ppermute | solution.py:22
  8.8 0.1 copy.75
  8.9 0.1 collective-permute-start.4
  9.0 0.1 copy.77
  9.2 0.1 copy.76
  9.3 0.0 copy-start.1
  9.3 4.4 %collective-permute-done = bf16[12,16,512]{2,0,1:T(8,128)(2,1)S(1)} collective-permute-done((bf16[12,16,512]{2,0,1:T(8,128)(2,1)S(1)}, bf16[12,16,512]{2,0,1:T(8,128)(2,1)S(1)}, u32[]{:S(2)}, u32[]{:S(2)}) %collective-permute-start) | collective-permute-done | bytes 196640 | tf_op jit(solution)/shard_map/ppermute | solution.py:22
  13.7 0.1 fusion.14
  13.9 0.1 pad_maximum_fusion
  14.0 3.5 %collective-permute-start.1 = (bf16[24,16,512]{2,0,1:T(8,128)(2,1)S(1)}, bf16[24,16,512]{2,0,1:T(8,128)(2,1)S(1)}, u32[]{:S(2)}, u32[]{:S(2)}) collective-permute-start(bf16[24,16,512]{2,0,1:T(8,128)(2,1)S(1)} %pad_maximum_fusion), channel_id=1, source_target_pairs={{0,224},{32,0},{64,32},{96,64},{128,96},{160,128},{192,160},{224,1... | collective-permute-start | bytes 1179656 | tf_op jit(solution)/shard_map/ppermute | solution.py:31
  17.5 0.0 collective-permute-done.4
  17.5 0.1 fusion.13
  17.6 0.1 pad_maximum_fusion.1
  17.7 0.1 collective-permute-start.5
  17.8 0.0 copy-done.1
  17.8 0.2 constant_dynamic-slice_fusion.3
  18.0 0.0 copy-start.3
  18.0 6.3 %collective-permute-done.1 = bf16[24,16,512]{2,0,1:T(8,128)(2,1)S(1)} collective-permute-done((bf16[24,16,512]{2,0,1:T(8,128)(2,1)S(1)}, bf16[24,16,512]{2,0,1:T(8,128)(2,1)S(1)}, u32[]{:S(2)}, u32[]{:S(2)}) %collective-permute-start.1) | collective-permute-done | bytes 393248 | tf_op jit(solution)/shard_map/ppermute | solution.py:31
  24.3 0.2 bitcast_add_fusion.3
  24.6 3.5 %collective-permute-start.2 = (bf16[24,16,512]{2,0,1:T(8,128)(2,1)S(1)}, bf16[24,16,512]{2,0,1:T(8,128)(2,1)S(1)}, u32[]{:S(2)}, u32[]{:S(2)}) collective-permute-start(bf16[24,16,512]{2,0,1:T(8,128)(2,1)S(1)} %bitcast_add_fusion.3), channel_id=1, source_target_pairs={{0,224},{32,0},{64,32},{96,64},{128,96},{160,128},{192,160},{224,1... | collective-permute-start | bytes 1179656 | tf_op jit(solution)/shard_map/ppermute | solution.py:31
  28.1 0.0 collective-permute-done.5
  28.1 0.2 bitcast_add_fusion.1
  28.3 0.1 collective-permute-start.6
  28.4 5.6 %collective-permute-done.2 = bf16[24,16,512]{2,0,1:T(8,128)(2,1)S(1)} collective-permute-done((bf16[24,16,512]{2,0,1:T(8,128)(2,1)S(1)}, bf16[24,16,512]{2,0,1:T(8,128)(2,1)S(1)}, u32[]{:S(2)}, u32[]{:S(2)}) %collective-permute-start.2) | collective-permute-done | bytes 393248 | tf_op jit(solution)/shard_map/ppermute | solution.py:31
  34.0 0.2 bitcast_add_fusion.2
  34.2 3.5 %collective-permute-start.3 = (bf16[24,16,512]{2,0,1:T(8,128)(2,1)S(1)}, bf16[24,16,512]{2,0,1:T(8,128)(2,1)S(1)}, u32[]{:S(2)}, u32[]{:S(2)}) collective-permute-start(bf16[24,16,512]{2,0,1:T(8,128)(2,1)S(1)} %bitcast_add_fusion.2), channel_id=1, source_target_pairs={{0,224},{32,0},{64,32},{96,64},{128,96},{160,128},{192,160},{224,1... | collective-permute-start | bytes 1179656 | tf_op jit(solution)/shard_map/ppermute | solution.py:31
  37.7 0.0 collective-permute-done.6
  37.7 0.2 bitcast_add_fusion
  38.0 0.1 collective-permute-start.7
  38.0 4.7 %collective-permute-done.3 = bf16[24,16,512]{2,0,1:T(8,128)(2,1)S(1)} collective-permute-done((bf16[24,16,512]{2,0,1:T(8,128)(2,1)S(1)}, bf16[24,16,512]{2,0,1:T(8,128)(2,1)S(1)}, u32[]{:S(2)}, u32[]{:S(2)}) %collective-permute-start.3) | collective-permute-done | bytes 393248 | tf_op jit(solution)/shard_map/ppermute | solution.py:31
  42.7 3.4 %collective-permute-done.7 = bf16[24,16,512]{2,0,1:T(8,128)(2,1)S(1)} collective-permute-done((bf16[24,16,512]{2,0,1:T(8,128)(2,1)S(1)}, bf16[24,16,512]{2,0,1:T(8,128)(2,1)S(1)}, u32[]{:S(2)}, u32[]{:S(2)}) %collective-permute-start.7) | collective-permute-done | bytes 393248 | tf_op jit(solution)/shard_map/ppermute | solution.py:32
  46.2 0.5 convolution_convert_fusion.1
  46.7 0.3 copy.38
  47.0 23.1 %all_to_all.10 = bf16[32,16,512]{2,1,0:T(8,128)(2,1)S(1)} all-to-all(bf16[32,16,512]{2,1,0:T(8,128)(2,1)S(1)} %copy.38), channel_id=1, replica_groups=mesh['rep'=8,'own'=32] {'own'}, dimensions={0} | all-to-all | bytes 1048576 | tf_op jit(solution)/shard_map/all_to_all | solution.py:47
  70.1 2.7 %multiply_reduce_fusion = (f32[]{:T(128)}, f32[512,512]{1,0:T(8,128)S(1)}) fusion(bf16[1,1,512,512]{3,2,1,0:T(8,128)(2,1)S(1)} %copy-done, bf16[512,512]{1,0:T(8,128)(2,1)S(1)} %bitcast.73, bf16[1,1,512,512]{3,2,1,0:T(8,128)(2,1)} %param.10), kind=kOutput, calls=%fused_computation.11 | convolution fusion | flops 537657344 | bytes 2621444 | tf_op jit(solution)/shard_map/dot_general | solution.py:50
  73.6 0.9 multiply_reduce_fusion.1
  75.1 0.9 multiply_convert_fusion
  76.0 3.7 %all-to-all-start.1 = ((bf16[32,16,512]{2,1,0:T(8,128)(2,1)}), bf16[32,16,512]{2,1,0:T(8,128)(2,1)S(1)}, u32[]{:S(2)}, u32[]{:S(2)}) async-start(bf16[32,16,512]{2,1,0:T(8,128)(2,1)} %bitcast.21), calls=%async_computation.1 | async-start | bytes 1048576 | tf_op jit(solution)/shard_map/all_to_all | solution.py:58
  79.7 0.0 copy-start.4
  79.7 1.4 %fusion.2 = f32[1,1,512,512]{3,2,1,0:T(8,128)} fusion(bf16[512,512]{1,0:T(8,128)(2,1)S(1)} %bitcast.74, f32[1,1,512,512]{3,2,1,0:T(8,128)S(1)} %copy-done.2), kind=kOutput, calls=%fused_computation.4 | convolution fusion | flops 269221888 | bytes 2621440 | tf_op jit(solution)/shard_map/ik,jk->ij/dot_general | solution.py:60
  81.2 0.0 copy-done.4
  81.2 1.5 %fusion.4 = f32[1,1,512,512]{3,2,1,0:T(8,128)} fusion(bf16[32,16,512]{2,1,0:T(8,128)(2,1)S(1)} %all_to_all.10, f32[1,1,512,512]{3,2,1,0:T(8,128)S(1)} %copy-done.4), kind=kOutput, calls=%fused_computation.6 | convolution fusion | flops 269221888 | bytes 2621440 | tf_op jit(solution)/shard_map/ki,kj->ij/dot_general | solution.py:61
  82.6 8.7 %all-to-all-done.1 = bf16[32,16,512]{2,1,0:T(8,128)(2,1)S(1)} async-done(((bf16[32,16,512]{2,1,0:T(8,128)(2,1)}), bf16[32,16,512]{2,1,0:T(8,128)(2,1)S(1)}, u32[]{:S(2)}, u32[]{:S(2)}) %all-to-all-start.1) | async-done | bytes 524320 | tf_op jit(solution)/shard_map/all_to_all | solution.py:58
  91.3 0.5 fusion.10
  91.8 1.3 %copy.42 = f32[24,16,512]{2,1,0:T(8,128)} copy(f32[24,16,512]{2,0,1:T(8,128)S(1)} %fusion.10) | data formatting | bytes 1572864
  (4 shorter events, 0.0 us)
Async XLA Ops:
  0.6 69.5 %copy-start = (bf16[1,1,512,512]{3,2,1,0:T(8,128)(2,1)S(1)}, bf16[1,1,512,512]{3,2,1,0:T(8,128)(2,1)}, u32[]{:S(2)}) copy-start(bf16[1,1,512,512]{3,2,1,0:T(8,128)(2,1)} %param.11) | copy-start | bytes 1572868
  2.3 11.5 %collective-permute-start = (bf16[12,16,512]{2,0,1:T(8,128)(2,1)S(1)}, bf16[12,16,512]{2,0,1:T(8,128)(2,1)S(1)}, u32[]{:S(2)}, u32[]{:S(2)}) collective-permute-start(bf16[12,16,512]{2,0,1:T(8,128)(2,1)S(1)} %bitcast.80), channel_id=1, source_target_pairs={{0,224},{32,0},{64,32},{96,64},{128,96},{160,128},{192,160},{224,1... | collective-permute-start | bytes 589832 | tf_op jit(solution)/shard_map/ppermute | solution.py:22
  8.9 8.6 %collective-permute-start.4 = (bf16[12,16,512]{2,0,1:T(8,128)(2,1)S(1)}, bf16[12,16,512]{2,0,1:T(8,128)(2,1)S(1)}, u32[]{:S(2)}, u32[]{:S(2)}) collective-permute-start(bf16[12,16,512]{2,0,1:T(8,128)(2,1)S(1)} %bitcast.79), channel_id=1, source_target_pairs={{0,32},{32,64},{64,96},{96,128},{128,160},{160,192},{192,224},{224... | collective-permute-start | bytes 589832 | tf_op jit(solution)/shard_map/ppermute | solution.py:23
  9.3 8.5 %copy-start.1 = (bf16[1,192,16,512]{3,2,1,0:T(8,128)(2,1)S(1)}, bf16[1,192,16,512]{3,2,1,0:T(8,128)(2,1)}, u32[]{:S(2)}) copy-start(bf16[1,192,16,512]{3,2,1,0:T(8,128)(2,1)} %param.6) | copy-start | bytes 9437188
  14.0 10.3 %collective-permute-start.1 = (bf16[24,16,512]{2,0,1:T(8,128)(2,1)S(1)}, bf16[24,16,512]{2,0,1:T(8,128)(2,1)S(1)}, u32[]{:S(2)}, u32[]{:S(2)}) collective-permute-start(bf16[24,16,512]{2,0,1:T(8,128)(2,1)S(1)} %pad_maximum_fusion), channel_id=1, source_target_pairs={{0,224},{32,0},{64,32},{96,64},{128,96},{160,128},{192,160},{224,1... | collective-permute-start | bytes 1179656 | tf_op jit(solution)/shard_map/ppermute | solution.py:31
  17.7 10.4 %collective-permute-start.5 = (bf16[24,16,512]{2,0,1:T(8,128)(2,1)S(1)}, bf16[24,16,512]{2,0,1:T(8,128)(2,1)S(1)}, u32[]{:S(2)}, u32[]{:S(2)}) collective-permute-start(bf16[24,16,512]{2,0,1:T(8,128)(2,1)S(1)} %pad_maximum_fusion.1), channel_id=1, source_target_pairs={{0,32},{32,64},{64,96},{96,128},{128,160},{160,192},{192,224},{224... | collective-permute-start | bytes 1179656 | tf_op jit(solution)/shard_map/ppermute | solution.py:32
  18.0 28.2 %copy-start.3 = (s32[24]{0:T(128)S(1)}, s32[24]{0:T(128)}, u32[]{:S(2)}) copy-start(s32[24]{0:T(128)} %param.7) | copy-start | bytes 292
  24.6 9.4 %collective-permute-start.2 = (bf16[24,16,512]{2,0,1:T(8,128)(2,1)S(1)}, bf16[24,16,512]{2,0,1:T(8,128)(2,1)S(1)}, u32[]{:S(2)}, u32[]{:S(2)}) collective-permute-start(bf16[24,16,512]{2,0,1:T(8,128)(2,1)S(1)} %bitcast_add_fusion.3), channel_id=1, source_target_pairs={{0,224},{32,0},{64,32},{96,64},{128,96},{160,128},{192,160},{224,1... | collective-permute-start | bytes 1179656 | tf_op jit(solution)/shard_map/ppermute | solution.py:31
  28.3 9.4 %collective-permute-start.6 = (bf16[24,16,512]{2,0,1:T(8,128)(2,1)S(1)}, bf16[24,16,512]{2,0,1:T(8,128)(2,1)S(1)}, u32[]{:S(2)}, u32[]{:S(2)}) collective-permute-start(bf16[24,16,512]{2,0,1:T(8,128)(2,1)S(1)} %bitcast_add_fusion.1), channel_id=1, source_target_pairs={{0,32},{32,64},{64,96},{96,128},{128,160},{160,192},{192,224},{224... | collective-permute-start | bytes 1179656 | tf_op jit(solution)/shard_map/ppermute | solution.py:32
  34.2 8.5 %collective-permute-start.3 = (bf16[24,16,512]{2,0,1:T(8,128)(2,1)S(1)}, bf16[24,16,512]{2,0,1:T(8,128)(2,1)S(1)}, u32[]{:S(2)}, u32[]{:S(2)}) collective-permute-start(bf16[24,16,512]{2,0,1:T(8,128)(2,1)S(1)} %bitcast_add_fusion.2), channel_id=1, source_target_pairs={{0,224},{32,0},{64,32},{96,64},{128,96},{160,128},{192,160},{224,1... | collective-permute-start | bytes 1179656 | tf_op jit(solution)/shard_map/ppermute | solution.py:31
  38.0 8.2 %collective-permute-start.7 = (bf16[24,16,512]{2,0,1:T(8,128)(2,1)S(1)}, bf16[24,16,512]{2,0,1:T(8,128)(2,1)S(1)}, u32[]{:S(2)}, u32[]{:S(2)}) collective-permute-start(bf16[24,16,512]{2,0,1:T(8,128)(2,1)S(1)} %bitcast_add_fusion), channel_id=1, source_target_pairs={{0,32},{32,64},{64,96},{96,128},{128,160},{160,192},{192,224},{224... | collective-permute-start | bytes 1179656 | tf_op jit(solution)/shard_map/ppermute | solution.py:32
  70.1 9.6 %copy-start.2 = (f32[1,1,512,512]{3,2,1,0:T(8,128)S(1)}, f32[1,1,512,512]{3,2,1,0:T(8,128)}, u32[]{:S(2)}) copy-start(f32[1,1,512,512]{3,2,1,0:T(8,128)} %param.8) | copy-start | bytes 3145732
  76.0 15.3 %all-to-all-start.1 = ((bf16[32,16,512]{2,1,0:T(8,128)(2,1)}), bf16[32,16,512]{2,1,0:T(8,128)(2,1)S(1)}, u32[]{:S(2)}, u32[]{:S(2)}) async-start(bf16[32,16,512]{2,1,0:T(8,128)(2,1)} %bitcast.21), calls=%async_computation.1 | async-start | bytes 1048576 | tf_op jit(solution)/shard_map/all_to_all | solution.py:58
  79.7 1.5 %copy-start.4 = (f32[1,1,512,512]{3,2,1,0:T(8,128)S(1)}, f32[1,1,512,512]{3,2,1,0:T(8,128)}, u32[]{:S(2)}) copy-start(f32[1,1,512,512]{3,2,1,0:T(8,128)} %param.9) | copy-start | bytes 3145732
